TPU v7x, 256 devices: a whole 4x4x8 slice. The times are simulated.
256 devices in a mesh: ctx: 32 (over x, y, core), sub: 8 (over z).
Axes of the slice: x: 4, y: 4, z: 8, core: 2. Of those that a mesh axis runs over, the one named last changes fastest.
Arguments:
- latent_cache: bfloat16 [8, 262144, 512], P(None, ('ctx', 'sub')), may hold values from -6 to 6
- rope_cache: bfloat16 [8, 64, 262144], P(None, None, ('ctx', 'sub')), may hold values from -5 to 5
- q_latent: bfloat16 [8, 2, 128, 512], P(None, None, 'sub'), may hold values from -12 to 12
- q_rope: bfloat16 [8, 2, 8192], P(None, None, 'sub'), may hold values from -12 to 12
- lengths: int32 [8], replicated, may hold values from 16384 to 262144, as said below
Outputs:
- context: bfloat16 [2048, 512], P(('ctx', 'sub'))
Inputs may be any that keep to these rules, and one draw needn't show every extreme that they name: `lengths`: the longest sequence has exactly 262144 cached positions.
All inputs are finite; a program needn't handle non-finite values.
Results may differ from a plain program's by a relative error of at most 0.0045.
Values may be sent and summed in bfloat16 or wider, within the bound.
A program may use at most 64 MiB of HBM per device.

v0:
```python
import jax
import jax.numpy as jnp
from jax import lax
from jax.sharding import PartitionSpec as P

NOPE = 128
QTOK = 2


def body(latent_cache, rope_cache, q_latent, q_rope, lengths):
    query_lat, query_rope = (
        lax.all_gather(q_latent, "sub", axis=2, tiled=True),
        lax.all_gather(q_rope, "sub", axis=2, tiled=True),
    )
    sequences, seq_dev, latent_width = latent_cache.shape
    rope_width = rope_cache.shape[1]
    head_count = query_lat.shape[2]
    row_count = QTOK * head_count
    score_scale = (NOPE + rope_width) ** (-0.5)
    query_lat = query_lat.reshape(sequences, row_count, latent_width)
    query_rope = query_rope.reshape(sequences, row_count, rope_width)
    scores = jnp.einsum("brl,bsl->brs", query_lat, latent_cache, preferred_element_type=jnp.float32)
    scores = scores + jnp.einsum(
        "brk,bks->brs", query_rope, rope_cache, preferred_element_type=jnp.float32
    )
    scores = scores * score_scale
    positions = lax.axis_index(("ctx", "sub")) * seq_dev + jnp.arange(seq_dev, dtype=jnp.int32)
    offsets = jnp.repeat(jnp.arange(QTOK, dtype=jnp.int32) - (QTOK - 1), head_count)
    visible_end = lengths[:, None] + offsets[None, :]
    visible = positions[None, None, :] < visible_end[:, :, None]
    local_top = jnp.max(jnp.where(visible, scores, -1e30), axis=2)
    row_top = lax.pmax(local_top, ("ctx", "sub"))
    weights = jnp.where(visible, jnp.exp(scores - row_top[:, :, None]), 0.0)
    denominator = jnp.sum(weights, axis=2).reshape(sequences * row_count)
    numerator = jnp.einsum(
        "brs,bsl->brl",
        weights.astype(jnp.bfloat16),
        latent_cache,
        preferred_element_type=jnp.float32,
    )
    numerator = numerator.reshape(sequences * row_count, latent_width)
    own_num, own_den = (
        lax.psum_scatter(numerator, ("ctx", "sub"), scatter_dimension=0, tiled=True),
        lax.psum_scatter(denominator, ("ctx", "sub"), scatter_dimension=0, tiled=True),
    )
    return (own_num / own_den[:, None]).astype(jnp.bfloat16)


def solution(mesh):
    in_specs = (
        P(None, ("ctx", "sub"), None),
        P(None, None, ("ctx", "sub")),
        P(None, None, "sub", None),
        P(None, None, "sub"),
        P(),
    )
    out_specs = P(("ctx", "sub"), None)
    return jax.shard_map(body, mesh=mesh, in_specs=in_specs, out_specs=out_specs, check_vma=False)
```

profile of v0, /device:TPU:1, one launch (start us, length us, event | category | flops | bytes accessed | tf_op | source)
XLA Modules:
  0.0 1413.0 jit_solution(3975872388298731802)
XLA Ops:
  6.5 0.0 copy-start
  6.5 0.0 all-gather.2.cloned.1.call-start
  6.5 0.7 all-gather.2.cloned.1.call-update
  7.3 0.0 reduce-scatter.2.cloned.1.call-start
  7.3 24.2 %all_gather.7 = bf16[8,2,8192]{2,1,0:T(2,128)(2,1)S(1)} all-gather(bf16[8,2,1024]{2,1,0:T(2,128)(2,1)} %param.8), channel_id=1, replica_groups=mesh['ctx'=32,'sub'=8] {'sub'}, dimensions={2}, use_global_device_ids=true | all-gather | bytes 294912 | tf_op jit(solution)/shard_map/all_gather | solution.py:13
  31.5 0.3 reshape.49
  31.9 0.1 broadcast_bitcast_fusion
  32.0 0.7 broadcast_add_fusion
  32.7 18.6 %all-gather.2.cloned.1.call-done = bf16[8,2,128,512]{3,2,1,0:T(8,128)(2,1)} async-done(((bf16[8,2,16,512]{3,2,1,0:T(8,128)(2,1)}), bf16[8,2,128,512]{3,2,1,0:T(8,128)(2,1)}) %all-gather.2.cloned.1.call-update) | async-done | bytes 2097168 | tf_op jit(solution)/shard_map/all_gather | solution.py:12
  51.4 6.4 fusion.10
  57.8 0.0 copy-done
  57.8 4.4 fusion
  62.2 77.8 %pmax.7 = f32[8,256]{1,0:T(8,128)S(1)} all-reduce(f32[8,256]{1,0:T(8,128)S(1)} %get-tuple-element.5), channel_id=1, replica_groups=mesh['ctx'=32,'sub'=8] {'ctx','sub'}, use_global_device_ids=true, to_apply=%region_1.2 | all-reduce | flops 2048 | bytes 16384 | tf_op jit(solution)/shard_map/pmax | solution.py:32
  140.0 9.2 fusion.3
  149.2 0.0 reduce-scatter.2.cloned.1.call-update
  149.2 4.5 fusion.1
  153.7 74.1 %all-reduce = f32[2048]{0:T(1024)S(1)} all-reduce(f32[2048]{0:T(1024)S(1)} %bitcast.14), channel_id=3, replica_groups=mesh['ctx'=32,'sub'=8] {'ctx','sub'}, use_global_device_ids=true, to_apply=%region_4.5.clone | all-reduce | flops 2048 | bytes 16384
  227.9 0.1 dynamic-slice
  227.9 1176.8 %reduce-scatter.2.cloned.1.call-done = f32[8,512]{1,0:T(8,128)} async-done(((f32[2048,512]{1,0:T(8,128)}), f32[8,512]{1,0:T(8,128)}) %reduce-scatter.2.cloned.1.call-update) | async-done | bytes 16400 | tf_op jit(solution)/shard_map/reduce_scatter | solution.py:43
  1404.7 1.4 divide_convert_fusion
  (3 shorter events, 0.0 us)
Async XLA Ops:
  6.5 51.2 %copy-start = (bf16[8,64,1024]{2,1,0:T(8,128)(2,1)S(1)}, bf16[8,64,1024]{2,1,0:T(8,128)(2,1)}, u32[]{:S(2)}) copy-start(bf16[8,64,1024]{2,1,0:T(8,128)(2,1)} %param.6) | copy-start | bytes 3145732
  6.5 44.8 %all-gather.2.cloned.1.call-start = ((), (), s32[]{:S(2)}) async-start(), calls=%async_computation.1 | async-start | bytes 2359296 | tf_op jit(solution)/shard_map/all_gather | solution.py:12
  7.3 1397.5 %reduce-scatter.2.cloned.1.call-start = ((), (), s32[]{:S(2)}) async-start(), calls=%async_computation.2 | async-start | bytes 4210688 | tf_op jit(solution)/shard_map/reduce_scatter | solution.py:43
Sparse Core Ops, SparseCore 0:
  9.2 42.1 all-gather.1
  149.3 1255.3 reduce-scatter.1
where the time goes:
time: 1430 us; the launch traced here: 1410 us
  waiting for transfers between devices  1200 us (84%)
  blocking collectives  176 us (12%)
  matrix products  19.9 us (1%)
    reduce_scatter x1, waiting for transfers between devices, body(): lax.psum_scatter(numerator, ('ctx', 'sub'), scatter_dimension=0, tiled=True)  1180 us
    pmax x1, blocking collectives, body(): row_top = lax.pmax(local_top, ('ctx', 'sub'))  77.8 us
    unnamed x1, blocking collectives  74.1 us
  transfers between devices with their start and end apart: 2, of which 2 were waited for; matrix products, arithmetic and copies ran while one was open for 0% of the time, Pallas kernels for 0%

commit v1 on v0

v1 whole, which is shorter than its diff:
```python
import functools

import jax
import jax.numpy as jnp
from jax import lax
from jax.experimental import pallas as pl
from jax.experimental.pallas import tpu as pltpu
from jax.sharding import PartitionSpec as P

MESH = pl.DeviceIdType.MESH
NOPE = 128
QTOK = 2
NX, NY, NC, NZ = 4, 4, 2, 8
LOG2E = 1.4426950408889634
FLOOR = -16384.0


def place():
    ctx = lax.axis_index("ctx")
    return ctx // (NY * NC), (ctx // NC) % NY, ctx % NC, lax.axis_index("sub")


def device(x, y, c, z):
    return ((x * NY + y) * NC + c, z)


def split3(v):
    hi = v.astype(jnp.bfloat16).astype(jnp.float32)
    rest = v - hi
    mid = rest.astype(jnp.bfloat16).astype(jnp.float32)
    return hi, mid, rest - mid


def lanes(shape):
    return lax.broadcasted_iota(jnp.int32, shape, len(shape) - 1)


def pack_rows(num, top, total):
    rows = num.shape[0]
    t1, t2, t3 = split3(top)
    l1, l2, _ = split3(total)
    lane = lanes((rows, 128))
    stats = jnp.where(
        lane < 16, t1, jnp.where(lane < 32, t2, jnp.where(lane < 48, t3, jnp.where(lane < 64, l1, l2)))
    )
    return jnp.concatenate([num.astype(jnp.bfloat16), stats.astype(jnp.bfloat16)], axis=1)


def unpack_rows(message):
    num = message[:, :512].astype(jnp.float32)
    stats = message[:, 512:].astype(jnp.float32)
    top = stats[:, 0:1] + stats[:, 16:17] + stats[:, 32:33]
    total = stats[:, 48:49] + stats[:, 64:65]
    return num, top, total


def merge(parts):
    top = functools.reduce(jnp.maximum, [p[1] for p in parts])
    factors = [jnp.exp2(p[1] - top) for p in parts]
    num = functools.reduce(jnp.add, [p[0] * f for p, f in zip(parts, factors)])
    total = functools.reduce(jnp.add, [p[2] * f for p, f in zip(parts, factors)])
    return num, top, total


def pack_owner(num, top, total):
    t1, t2, t3 = split3(top)
    l1, l2, _ = split3(total)
    lane = lanes((64, 128))
    tops = jnp.where(lane < 16, t1, jnp.where(lane < 32, t2, t3)).reshape(8, 8, 128)
    totals = jnp.where(lane < 16, l1, l2).reshape(8, 8, 128)
    num = num.reshape(8, 8, 512)
    left = jnp.concatenate([num[:, :, :256], tops], axis=2)
    right = jnp.concatenate([num[:, :, 256:], totals], axis=2)
    return jnp.concatenate([left, right], axis=1).astype(jnp.bfloat16)


def kernel(
    lat_hbm, rope_hbm, q_hbm, qr_hbm, lengths, out,
    kv, rr, q, qr, num, core_in, x_out, x_in, y_out, y_in, z_out, z_in,
    kv_sem, own_sem, zq_send, zq_recv, rz_send, rz_recv, yq_send, yq_recv, rx_send, rx_recv,
    cq_send, cq_recv, cr_send, cr_recv, ce_send, ce_recv, x_send, x_recv, y_send, y_recv, z_send, z_recv,
):
    x, y, c, z = place()
    positions = kv.shape[1]
    first = ((x * NY + y) * NC + c) * NZ * positions + z * positions
    scale = (NOPE + 64) ** -0.5 * LOG2E
    my_j = y // 2

    def wrap_x(d):
        return (x + d) % NX

    def wrap_y(d):
        return (y + d) % NY

    def wrap_z(d):
        return (z + d) % NZ

    def step_dx(k):
        return jnp.where(k < 2, 2, jnp.where(k >= 6, 0, jnp.where(k % 2 == 0, 1, 3)))

    def step_j(k):
        early = jnp.where(k < 2, k, jnp.where(k < 4, 0, 1))
        return jnp.where(k < 6, early, jnp.where(k == 6, 1 - my_j, my_j))

    def step_seq(k):
        return wrap_x(step_dx(k)) * 2 + step_j(k)

    def load_kv(k):
        b = step_seq(k)
        return (
            pltpu.make_async_copy(lat_hbm.at[b], kv.at[k], kv_sem.at[k, 0]),
            pltpu.make_async_copy(rope_hbm.at[b], rr.at[k, pl.ds(0, 64)], kv_sem.at[k, 1]),
            pltpu.make_async_copy(rope_hbm.at[b], rr.at[k, pl.ds(64, 64)], kv_sem.at[k, 2]),
        )

    def remote(src, dst, send, recv, target):
        return pltpu.make_async_remote_copy(
            src_ref=src, dst_ref=dst, send_sem=send, recv_sem=recv, device_id=target, device_id_type=MESH
        )

    tile = pl.ds(pl.multiple_of(y * 128, 128), 128)

    own_q = pltpu.make_async_copy(q_hbm.at[:, c, :, tile], q.at[:, z, c, :, tile], own_sem.at[0])
    own_r = pltpu.make_async_copy(qr_hbm.at[2 * x + c], qr.at[c, x, z], own_sem.at[1])

    def zq(b, d):
        return remote(
            q_hbm.at[b, c, :, tile], q.at[b, z, c, :, tile], zq_send.at[b, d - 1], zq_recv.at[b, d - 1],
            device(x, y, c, wrap_z(d)),
        )

    def rz(d):
        return remote(
            qr_hbm.at[2 * x + c], qr.at[c, x, z], rz_send.at[d - 1], rz_recv.at[d - 1], device(x, y, c, wrap_z(d))
        )

    def yq(b, d):
        return remote(
            q.at[b, :, c, :, tile], q.at[b, :, c, :, tile], yq_send.at[b, d - 1], yq_recv.at[b, d - 1],
            device(x, wrap_y(d), c, z),
        )

    def rx(d):
        return remote(qr.at[c, x], qr.at[c, x], rx_send.at[d - 1], rx_recv.at[d - 1], device(wrap_x(d), y, c, z))

    def cq(b):
        return remote(q.at[b, :, c], q.at[b, :, c], cq_send.at[b], cq_recv.at[b], device(x, y, 1 - c, z))

    def cr():
        return remote(qr.at[c], qr.at[c], cr_send, cr_recv, device(x, y, 1 - c, z))

    def ce(k):
        return remote(num.at[k, 1 - c], core_in.at[k], ce_send.at[k], ce_recv.at[k], device(x, y, 1 - c, z))

    def xs(k):
        d = step_dx(k)
        j = step_j(k)
        return remote(
            x_out.at[k], x_in.at[d - 1, j], x_send.at[k], x_recv.at[d - 1, j], device(wrap_x(d), y, c, z)
        )

    def xr(d, j):
        return remote(
            x_out.at[0], x_in.at[d - 1, j], x_send.at[0], x_recv.at[d - 1, j], device(wrap_x(d), y, c, z)
        )

    def ys(t):
        return remote(
            y_out.at[t], y_in.at[y % 2], y_send.at[t], y_recv.at[y % 2], device(x, (1 - my_j) * 2 + t, c, z)
        )

    def yr(s):
        return remote(
            y_out.at[s], y_in.at[s], y_send.at[s], y_recv.at[s], device(x, (1 - my_j) * 2 + s, c, z)
        )

    y_pair = my_j * 2 + (1 - y % 2)

    def zs(column, d):
        return remote(
            z_out.at[column, wrap_z(d)], z_in.at[column, z], z_send.at[column, d], z_recv.at[column, d],
            device(x, jnp.where(column == 0, y, y_pair), c, wrap_z(d)),
        )

    def zr(column, d):
        source = (z - d + NZ) % NZ
        return remote(
            z_out.at[column, z], z_in.at[column, source], z_send.at[column, d], z_recv.at[column, d],
            device(x, y_pair, c, wrap_z(d)),
        )

    for k in range(2):
        for copy in load_kv(k):
            copy.start()
    own_q.start()
    own_r.start()
    partners = [device(x, y, 1 - c, z)]
    partners += [device(wrap_x(d), y, c, z) for d in (1, 2, 3)]
    partners += [device(x, (1 - my_j) * 2 + t, c, z) for t in (0, 1)]
    partners += [device(x, y, c, wrap_z(d)) for d in range(1, NZ)]
    partners += [device(x, y_pair, c, wrap_z(d)) for d in range(NZ)]
    barrier = pltpu.get_barrier_semaphore()
    for partner in partners:
        pl.semaphore_signal(barrier, inc=1, device_id=partner, device_id_type=MESH)

    def load_rest(k, carry):
        for copy in load_kv(k):
            copy.start()
        return carry

    lax.fori_loop(2, 8, load_rest, 0)
    pl.semaphore_wait(barrier, len(partners))

    z_order = (4, 3, 5, 2, 6, 1, 7)
    for d in z_order:
        rz(d).start()

    def send_z(k, carry):
        b = step_seq(k)
        for d in z_order:
            zq(b, d).start()
        return carry

    lax.fori_loop(0, 8, send_z, 0)
    own_r.wait()
    own_q.wait()

    for d in z_order:
        rz(d).wait_recv()
    for d in (2, 1, 3):
        rx(d).start()

    def send_y(k, carry):
        b = step_seq(k)
        for d in z_order:
            zq(b, d).wait_recv()
        for d in (2, 1, 3):
            yq(b, d).start()
        return carry

    lax.fori_loop(0, 8, send_y, 0)
    for d in (1, 2, 3):
        rx(d).wait_recv()
    cr().start()

    def send_core(k):
        b = step_seq(k)
        for d in (1, 2, 3):
            yq(b, d).wait_recv()
        cq(b).start()

    send_core(0)
    cr().wait_recv()

    rows_q = (NZ, QTOK, 16)

    def compute(k):
        b = step_seq(k)
        cq(b).wait_recv()
        for copy in load_kv(k):
            copy.wait()
        query = q[b].reshape(256, 512)
        rope_q = qr[b % 2, b // 2]
        half = lanes((NZ, 16, 128)) // 64
        zero = jnp.zeros_like(rope_q)
        rope_q = jnp.stack([jnp.where(half == t, rope_q, zero) for t in range(QTOK)], axis=1).reshape(256, 128)
        latent = kv[k]
        scores = lax.dot_general(query, latent, (((1,), (1,)), ((), ())), preferred_element_type=jnp.float32)
        scores = scores + jnp.dot(rope_q, rr[k], preferred_element_type=jnp.float32)
        position = first + lanes((1, positions))
        bias = jnp.concatenate(
            [jnp.where(position < lengths[b] - (QTOK - 1 - t), 0.0, -1e30) for t in range(QTOK)], axis=0
        )
        scores = scores.reshape(*rows_q, positions) * scale + bias.reshape(1, QTOK, 1, positions)
        scores = scores.reshape(256, positions)
        top = jnp.maximum(jnp.max(scores, axis=1, keepdims=True), FLOOR)
        weights = jnp.exp2(scores - top)
        total = jnp.sum(weights, axis=1, keepdims=True)
        part = jnp.dot(weights.astype(jnp.bfloat16), latent, preferred_element_type=jnp.float32)
        stats = jnp.where(lanes((256, 128)) < 64, top, total)
        num[k, :, :, 0:512] = part.reshape(2, 128, 512)
        num[k, :, :, 512:640] = stats.reshape(2, 128, 128)
        ce(k).start()

    def core_merged(k):
        ce(k).wait_recv()
        mine = num[k, c]
        other = core_in[k]
        return merge([(a[:, :512], a[:, 512:513], a[:, 576:577]) for a in (mine, other)])

    def step(k, carry):
        send_core(k + 1)
        compute(k)

        @pl.when(k >= 1)
        def _():
            x_out[k - 1] = pack_rows(*core_merged(k - 1))
            xs(k - 1).start()

        return carry

    lax.fori_loop(0, 7, step, 0)
    compute(7)

    def own_pair(k, j):
        parts = [core_merged(k)]
        for d in (2, 1, 3):
            xr(d, j).wait_recv()
            parts.append(unpack_rows(x_in[d - 1, j]))
        return merge(parts)

    def token(a, t):
        return a.reshape(4, QTOK, 16, a.shape[1])[:, t].reshape(64, a.shape[1])

    merged = own_pair(6, 1 - my_j)
    for t in range(QTOK):
        y_out[t] = pack_rows(*[token(a, t) for a in merged])
        ys(t).start()

    merged = own_pair(7, my_j)
    mine = y % 2
    tokens = [[token(a, t) for a in merged] for t in range(QTOK)]
    other = [jnp.where(mine == 0, b, a) for a, b in zip(*tokens)]
    z_out[1] = pack_owner(*other)
    for d in (4, 3, 5, 2, 6, 1, 7, 0):
        zs(1, d).start()
    parts = [tuple(jnp.where(mine == 0, a, b) for a, b in zip(*tokens))]
    for s in range(2):
        yr(s).wait_recv()
        parts.append(unpack_rows(y_in[s]))
    z_out[0] = pack_owner(*merge(parts))
    for d in z_order:
        zs(0, d).start()
    z_in[0, z] = z_out[0, z]
    for d in range(1, NZ):
        zr(0, d).wait_recv()
    for d in range(NZ):
        zr(1, d).wait_recv()

    got = z_in[...].reshape(16, 16, 384).astype(jnp.float32)
    tops = got[:, :8, 256:]
    totals = got[:, 8:, 256:]
    tops = tops[:, :, 0:1] + tops[:, :, 16:17] + tops[:, :, 32:33]
    totals = totals[:, :, 0:1] + totals[:, :, 16:17]
    top = jnp.max(tops, axis=0, keepdims=True)
    factor = jnp.exp2(tops - top)
    total = jnp.sum(totals * factor, axis=0)
    left = jnp.sum(got[:, :8, :256] * factor, axis=0)
    right = jnp.sum(got[:, 8:, :256] * factor, axis=0)
    out[...] = (jnp.concatenate([left, right], axis=1) / total).astype(jnp.bfloat16)

    for d in range(1, NZ):
        rz(d).wait_send()
        zs(0, d).wait_send()
    for d in range(NZ):
        zs(1, d).wait_send()
    for d in (1, 2, 3):
        rx(d).wait_send()
    cr().wait_send()
    for t in range(QTOK):
        ys(t).wait_send()

    def drain(k, carry):
        for d in range(1, NZ):
            zq(k, d).wait_send()
        for d in (1, 2, 3):
            yq(k, d).wait_send()
        cq(k).wait_send()
        ce(k).wait_send()
        return carry

    lax.fori_loop(0, 8, drain, 0)

    def drain_x(k, carry):
        xs(k).wait_send()
        return carry

    lax.fori_loop(0, 6, drain_x, 0)


def body(latent_cache, rope_cache, q_latent, q_rope, lengths):
    batch, positions, width = latent_cache.shape
    heads = q_latent.shape[2]
    rope_q = q_rope.reshape(batch, QTOK, heads, 64).transpose(0, 2, 1, 3).reshape(batch, heads, 128)
    anywhere = pl.BlockSpec(memory_space=pl.ANY)
    dma = pltpu.SemaphoreType.DMA
    return pl.pallas_call(
        kernel,
        out_shape=jax.ShapeDtypeStruct((8, width), jnp.bfloat16),
        in_specs=[anywhere] * 4 + [pl.BlockSpec(memory_space=pltpu.SMEM)],
        out_specs=pl.BlockSpec(memory_space=pltpu.VMEM),
        scratch_shapes=[
            pltpu.VMEM((8, positions, width), jnp.bfloat16),
            pltpu.VMEM((8, 128, positions), jnp.bfloat16),
            pltpu.VMEM((8, NZ, QTOK, 16, width), jnp.bfloat16),
            pltpu.VMEM((2, 4, NZ, 16, 128), jnp.bfloat16),
            pltpu.VMEM((8, 2, 128, 640), jnp.float32),
            pltpu.VMEM((8, 128, 640), jnp.float32),
            pltpu.VMEM((6, 128, 640), jnp.bfloat16),
            pltpu.VMEM((3, 2, 128, 640), jnp.bfloat16),
            pltpu.VMEM((2, 64, 640), jnp.bfloat16),
            pltpu.VMEM((2, 64, 640), jnp.bfloat16),
            pltpu.VMEM((2, 8, 16, 384), jnp.bfloat16),
            pltpu.VMEM((2, 8, 16, 384), jnp.bfloat16),
            dma((8, 3)), dma((2,)),
            dma((8, 7)), dma((8, 7)), dma((7,)), dma((7,)),
            dma((8, 3)), dma((8, 3)), dma((3,)), dma((3,)),
            dma((8,)), dma((8,)), dma, dma,
            dma((8,)), dma((8,)),
            dma((6,)), dma((3, 2)), dma((2,)), dma((2,)),
            dma((2, 8)), dma((2, 8)),
        ],
        compiler_params=pltpu.CompilerParams(
            collective_id=0, has_side_effects=True, vmem_limit_bytes=56 * 2**20
        ),
        cost_estimate=pl.CostEstimate(flops=5 * 10**9, bytes_accessed=10 * 10**6, transcendentals=2 * 10**6),
    )(latent_cache, rope_cache, q_latent, rope_q, lengths)


def solution(mesh):
    in_specs = (
        P(None, ("ctx", "sub"), None),
        P(None, None, ("ctx", "sub")),
        P(None, None, "sub", None),
        P(None, None, "sub"),
        P(),
    )
    out_specs = P(("ctx", "sub"), None)
    return jax.shard_map(body, mesh=mesh, in_specs=in_specs, out_specs=out_specs, check_vma=False)
```

time: 1430 us -> 60 us (0.04)
  the two profiles are of different devices: /device:TPU:1 before, /device:TPU:24 now
where the time goes in v1:
time: 60 us; the launch traced here: 59.8 us
  Pallas kernels  56.9 us (95%)
  local copies, waits for them, and re-layouts  2.91 us (5%)
    pallas_call x1, Pallas kernels, body(): pl.pallas_call(kernel, out_shape=jax.ShapeDtypeStruct((8, width), jnp.bfl...  56.9 us
    reshape x3, local copies, waits for them, and re-layouts, body(): q_rope.reshape(batch, QTOK, heads, 64).transpose(0, 2, 1, 3)  1.62 us
    unnamed x1, local copies, waits for them, and re-layouts  1.3 us

profile of v1, /device:TPU:24, one launch (start us, length us, event | category | flops | bytes accessed | tf_op | source)
XLA Modules:
  0.0 59.8 jit_solution(13511248950017350552)
XLA Ops:
  0.0 0.9 %reshape.6 = bf16[8,2,16,64]{3,2,1,0:T(8,128)(2,1)S(1)} reshape(bf16[8,2,1024]{2,1,0:T(2,128)(2,1)} %param.8) | data formatting | bytes 65536 | tf_op jit(solution)/shard_map/reshape | solution.py:384
  0.9 0.1 copy.8
  0.9 0.7 %reshape.7.qr_hbm = bf16[8,16,128]{2,1,0:T(8,128)(2,1)} reshape(bf16[8,16,2,64]{3,2,1,0:T(2,128)(2,1)S(1)} %bitcast.3) | data formatting | bytes 65536 | tf_op jit(solution)/shard_map/reshape | solution.py:384
  1.6 56.9 %shard_map.55 = bf16[8,512]{1,0:T(8,128)(2,1)} custom-call(bf16[8,1024,512]{2,1,0:T(8,128)(2,1)} %lat_hbm.1, bf16[8,64,1024]{2,1,0:T(8,128)(2,1)} %rope_hbm.1, bf16[8,2,16,512]{3,2,1,0:T(8,128)(2,1)} %q_hbm.1, bf16[8,16,128]{2,1,0:T(8,128)(2,1)} %reshape.7.qr_hbm, s32[8]{0:T(128)} %lengths.1), custom_call_target="tpu_custom_call" | custom-call | flops 5000000000 | bytes 10000000 | tf_op jit(solution)/shard_map/pallas_call | solution.py:387
  58.5 1.3 %copy.10 = bf16[8,512]{1,0:T(8,128)(2,1)} copy(bf16[8,512]{1,0:T(8,128)(2,1)} %shard_map.55) | data formatting | bytes 16384

commit v2 on v1

v2 whole, which is shorter than its diff:
```python
import functools

import jax
import jax.numpy as jnp
from jax import lax
from jax.experimental import pallas as pl
from jax.experimental.pallas import tpu as pltpu
from jax.sharding import PartitionSpec as P

MESH = pl.DeviceIdType.MESH
NOPE = 128
QTOK = 2
NX, NY, NC, NZ = 4, 4, 2, 8
LOG2E = 1.4426950408889634
FLOOR = -16384.0


def place():
    ctx = lax.axis_index("ctx")
    return ctx // (NY * NC), (ctx // NC) % NY, ctx % NC, lax.axis_index("sub")


def device(x, y, c, z):
    return ((x * NY + y) * NC + c, z)


def iota(shape, axis):
    return lax.broadcasted_iota(jnp.int32, shape, axis)


def lanes(shape):
    return iota(shape, len(shape) - 1)


def to_row(column, offset=0):
    shape = (column.shape[0], 128)
    return jnp.sum(jnp.where(lanes(shape) == iota(shape, 0) + offset, column, 0.0), axis=0, keepdims=True)


def to_column(row, rows, offset=0):
    shape = (rows, 128)
    return jnp.sum(jnp.where(lanes(shape) == iota(shape, 0) + offset, row, 0.0), axis=1, keepdims=True)


def merge(parts):
    top = functools.reduce(jnp.maximum, [p[1] for p in parts])
    factors = [jnp.exp2(p[1] - top) for p in parts]
    num = functools.reduce(jnp.add, [p[0] * f for p, f in zip(parts, factors)])
    total = functools.reduce(jnp.add, [p[2] * f for p, f in zip(parts, factors)])
    return num, top, total


class Pair:
    def __init__(self, *copies):
        self.copies = copies

    def start(self):
        for copy in self.copies:
            copy.start()

    def wait_send(self):
        for copy in self.copies:
            copy.wait_send()

    def wait_recv(self):
        for copy in self.copies:
            copy.wait_recv()


def kernel(
    lat_hbm, rope_hbm, q_hbm, qr_hbm, lengths, out,
    kv, rr, q, qr_in, qr, num, core_in,
    x_out, x_ost, x_in, x_ist, y_out, y_ost, y_in, y_ist, v_out, v_ost, v_in, v_ist,
    w_out, w_ost, w_in, w_ist, z_out, z_ost, z_in, z_ist,
    kv_sem, own_sem, zq_send, zq_recv, rz_send, rz_recv, pq_send, pq_recv, rx_send, rx_recv,
    cq_send, cq_recv, cr_send, cr_recv, ce_send, ce_recv,
    x_send, x_recv, y_send, y_recv, v_send, v_recv, w_send, w_recv, z_send, z_recv,
):
    x, y, c, z = place()
    positions = kv.shape[1]
    first = (((x * NY + y) * NC + c) * NZ + z) * positions
    scale = (NOPE + 64) ** -0.5 * LOG2E
    my_j = y // 2
    y_pair = my_j * 2 + (1 - y % 2)

    def wrap_x(d):
        return (x + d) % NX

    def wrap_y(d):
        return (y + d) % NY

    def wrap_z(d):
        return (z + d) % NZ

    def step_dx(k):
        return jnp.where(k < 2, 2, jnp.where(k >= 6, 0, jnp.where(k % 2 == 0, 1, 3)))

    def step_j(k):
        late = (k == 4) | (k == 5) | (k == 7)
        return jnp.where(k < 2, k, jnp.where(late, my_j, 1 - my_j))

    def step_pair(k):
        return wrap_x(step_dx(k))

    def load_kv(k):
        b = step_pair(k) * 2 + step_j(k)
        return (
            pltpu.make_async_copy(lat_hbm.at[b], kv.at[k], kv_sem.at[k, 0]),
            pltpu.make_async_copy(rope_hbm.at[b], rr.at[k, pl.ds(0, 64)], kv_sem.at[k, 1]),
            pltpu.make_async_copy(rope_hbm.at[b], rr.at[k, pl.ds(64, 64)], kv_sem.at[k, 2]),
        )

    def remote(src, dst, send, recv, target):
        return pltpu.make_async_remote_copy(
            src_ref=src, dst_ref=dst, send_sem=send, recv_sem=recv, device_id=target, device_id_type=MESH
        )

    def lane_tile(i):
        return pl.ds(pl.multiple_of(i * 128, 128), 128)

    tiles = (lane_tile(y), lane_tile(x))

    own_q = [
        pltpu.make_async_copy(q_hbm.at[:, j, c, :, tiles[j]], q.at[:, j, z, c, :, tiles[j]], own_sem.at[j])
        for j in range(2)
    ]
    own_r = pltpu.make_async_copy(qr_hbm.at[2 * x + c], qr_in, own_sem.at[2])

    def zq(p, j, d):
        return remote(
            q_hbm.at[p, j, c, :, tiles[j]], q.at[p, j, z, c, :, tiles[j]],
            zq_send.at[p, j, d - 1], zq_recv.at[p, j, d - 1], device(x, y, c, wrap_z(d)),
        )

    def rz(d):
        return remote(
            qr.at[c, x, z], qr.at[c, x, z], rz_send.at[d - 1], rz_recv.at[d - 1], device(x, y, c, wrap_z(d))
        )

    def pq(p, j, d):
        target = device(x, wrap_y(d), c, z) if j == 0 else device(wrap_x(d), y, c, z)
        return remote(
            q.at[p, j, :, c, :, tiles[j]], q.at[p, j, :, c, :, tiles[j]],
            pq_send.at[p, j, d - 1], pq_recv.at[p, j, d - 1], target,
        )

    def pq_wait(p, j, d):
        piece = q.at[p, j, :, c, :, pl.ds(0, 128)]
        return remote(
            piece, piece, pq_send.at[p, j, d - 1], pq_recv.at[p, j, d - 1], device(x, wrap_y(d), c, z)
        )

    def rx(d):
        return remote(qr.at[c, x], qr.at[c, x], rx_send.at[d - 1], rx_recv.at[d - 1], device(wrap_x(d), y, c, z))

    def cq(p, j):
        return remote(
            q.at[p, j, :, c], q.at[p, j, :, c], cq_send.at[p, j], cq_recv.at[p, j], device(x, y, 1 - c, z)
        )

    def cr():
        return remote(qr.at[c], qr.at[c], cr_send, cr_recv, device(x, y, 1 - c, z))

    def ce(k):
        return remote(num.at[k, 1 - c], core_in.at[k], ce_send.at[k], ce_recv.at[k], device(x, y, 1 - c, z))

    def xs(k):
        side = k % 2
        j = step_j(k)
        target = device(wrap_x(1 + 2 * side), y, c, z)
        return Pair(
            remote(x_out.at[k - 2], x_in.at[side, j], x_send.at[0, k - 2], x_recv.at[0, side, j], target),
            remote(x_ost.at[k - 2], x_ist.at[side, j], x_send.at[1, k - 2], x_recv.at[1, side, j], target),
        )

    def xr(side, j):
        target = device(wrap_x(1), y, c, z)
        return Pair(
            remote(x_out.at[0], x_in.at[side, j], x_send.at[0, 0], x_recv.at[0, side, j], target),
            remote(x_ost.at[0], x_ist.at[side, j], x_send.at[1, 0], x_recv.at[1, side, j], target),
        )

    def ys(d):
        target = device(x, wrap_y(d), c, z)
        unit = wrap_y(d)
        return Pair(
            remote(y_out.at[unit], y_in.at[d - 1], y_send.at[0, d - 1], y_recv.at[0, d - 1], target),
            remote(y_ost.at[unit], y_ist.at[d - 1], y_send.at[1, d - 1], y_recv.at[1, d - 1], target),
        )

    def vs():
        target = device(wrap_x(2), y, c, z)
        return Pair(
            remote(v_out, v_in, v_send.at[0], v_recv.at[0], target),
            remote(v_ost, v_ist, v_send.at[1], v_recv.at[1], target),
        )

    def ws(t):
        target = device(x, (1 - my_j) * 2 + t, c, z)
        slot = y % 2
        return Pair(
            remote(w_out.at[t], w_in.at[slot], w_send.at[0, t], w_recv.at[0, slot], target),
            remote(w_ost.at[t], w_ist.at[slot], w_send.at[1, t], w_recv.at[1, slot], target),
        )

    def wr(s):
        target = device(x, (1 - my_j) * 2 + s, c, z)
        return Pair(
            remote(w_out.at[s], w_in.at[s], w_send.at[0, s], w_recv.at[0, s], target),
            remote(w_ost.at[s], w_ist.at[s], w_send.at[1, s], w_recv.at[1, s], target),
        )

    def zs(column, d):
        target = device(x, y if column == 0 else y_pair, c, wrap_z(d))
        there = wrap_z(d)
        return Pair(
            remote(z_out.at[column, there], z_in.at[column, z], z_send.at[0, column, d], z_recv.at[0, column, d], target),
            remote(z_ost.at[column, there], z_ist.at[column, z], z_send.at[1, column, d], z_recv.at[1, column, d], target),
        )

    def zr(column, d):
        source = (z - d + NZ) % NZ
        target = device(x, y_pair, c, wrap_z(d))
        return Pair(
            remote(z_out.at[column, z], z_in.at[column, source], z_send.at[0, column, d], z_recv.at[0, column, d], target),
            remote(z_ost.at[column, z], z_ist.at[column, source], z_send.at[1, column, d], z_recv.at[1, column, d], target),
        )

    partners = [device(x, y, c, wrap_z(d)) for d in range(1, NZ)]
    partners += [device(wrap_x(d), y, c, z) for d in (1, 2, 3)]
    partners += [device(x, wrap_y(d), c, z) for d in (1, 2, 3)]
    partners += [device(x, y, 1 - c, z)]
    barrier = pltpu.get_barrier_semaphore()
    for partner in partners:
        pl.semaphore_signal(barrier, inc=1, device_id=partner, device_id_type=MESH)
    own_r.start()
    for copy in own_q:
        copy.start()

    def load(k, carry):
        for copy in load_kv(k):
            copy.start()
        return carry

    lax.fori_loop(0, 8, load, 0)
    own_r.wait()
    spread = (lanes((16, 1024)) // 64) == iota((16, 1024), 0)
    head = iota((16, 128), 0)
    own_rope = jnp.zeros((16, 128), jnp.float32)
    raw = qr_in[...].astype(jnp.float32)
    for t in range(QTOK):
        wide = jnp.where(spread, raw[t : t + 1], 0.0)
        narrow = functools.reduce(jnp.add, [wide[:, i * 128 : (i + 1) * 128] for i in range(8)])
        own_rope = own_rope + jnp.where(head % 2 == t, narrow, pltpu.roll(narrow, 64, 1))
    qr[c, x, z] = own_rope.astype(jnp.bfloat16)
    pl.semaphore_wait(barrier, len(partners))

    z_order = (4, 3, 5, 2, 6, 1, 7)
    pair_order = (2, 1, 3, 0)
    for d in z_order:
        rz(d).start()

    def send_z(p, j):
        for d in z_order:
            zq(p, j, d).start()

    def wait_z(p, j):
        for d in z_order:
            zq(p, j, d).wait_recv()

    send_z(wrap_x(2), 0)
    for dx in pair_order:
        send_z(wrap_x(dx), 1)
    for dx in pair_order[1:]:
        send_z(wrap_x(dx), 0)
    for copy in own_q:
        copy.wait()

    for d in z_order:
        rz(d).wait_recv()
    for d in (2, 1, 3):
        rx(d).start()
    wait_z(wrap_x(2), 0)
    for d in (2, 1, 3):
        pq(wrap_x(2), 0, d).start()
    for dx in pair_order:
        wait_z(wrap_x(dx), 1)
    for dx in pair_order:
        for d in (2, 1, 3):
            pq(wrap_x(d + dx), 1, d).start()
    for dx in pair_order[1:]:
        wait_z(wrap_x(dx), 0)
        for d in (2, 1, 3):
            pq(wrap_x(dx), 0, d).start()

    def send_core(k):
        p, j = step_pair(k), step_j(k)
        for d in (1, 2, 3):
            pq_wait(p, j, d).wait_recv()
        cq(p, j).start()

    send_core(0)
    for d in (1, 2, 3):
        rx(d).wait_recv()
    cr().start()

    def compute(k):
        p, j = step_pair(k), step_j(k)
        cq(p, j).wait_recv()
        for copy in load_kv(k):
            copy.wait()
        query = q[p, j].reshape(256, 512)
        rope_q = qr[j, p]
        half = lanes((NZ, 16, 128)) // 64
        zero = jnp.zeros_like(rope_q)
        rope_q = jnp.stack([jnp.where(half == t, rope_q, zero) for t in range(QTOK)], axis=1).reshape(256, 128)
        latent = kv[k]
        scores = lax.dot_general(query, latent, (((1,), (1,)), ((), ())), preferred_element_type=jnp.float32)
        scores = scores + jnp.dot(rope_q, rr[k], preferred_element_type=jnp.float32)
        position = first + lanes((1, positions))
        length = lengths[p * 2 + j]
        bias = jnp.concatenate(
            [jnp.where(position < length - (QTOK - 1 - t), 0.0, -1e30) for t in range(QTOK)], axis=0
        )
        scores = scores.reshape(NZ, QTOK, 16, positions) * scale + bias.reshape(1, QTOK, 1, positions)
        scores = scores.reshape(256, positions)
        top = jnp.maximum(jnp.max(scores, axis=1, keepdims=True), FLOOR)
        weights = jnp.exp2(scores - top)
        total = jnp.sum(weights, axis=1, keepdims=True)
        part = jnp.dot(weights.astype(jnp.bfloat16), latent, preferred_element_type=jnp.float32)
        stats = jnp.where(lanes((256, 128)) < 64, top, total)
        num[k, :, :, 0:512] = part.reshape(2, 128, 512)
        num[k, :, :, 512:640] = stats.reshape(2, 128, 128)
        ce(k).start()

    def core_merged(k):
        ce(k).wait_recv()
        return merge([(a[:, :512], a[:, 512:513], a[:, 576:577]) for a in (num[k, c], core_in[k])])

    def token(a, t):
        return a.reshape(4, QTOK, 16, a.shape[1])[:, t].reshape(64, a.shape[1])

    def half_rows(merged, t):
        rows, top, total = [token(a, t) for a in merged]
        return rows.astype(jnp.bfloat16), to_row(top) + to_row(total, 64)

    def half_parts(rows, stats):
        return rows.astype(jnp.float32), to_column(stats, 64), to_column(stats, 64, 64)

    def route_y(k):
        merged = core_merged(k)
        for t in range(QTOK):
            unit = 2 * k + t
            y_out[unit], y_ost[unit] = half_rows(merged, t)

            @pl.when(unit != y)
            def _():
                ys((unit - y + NY) % NY).start()

    def route_x(k):
        rows, top, total = core_merged(k)
        x_out[k - 2] = rows.astype(jnp.bfloat16)
        x_ost[k - 2, 0] = to_row(top)
        x_ost[k - 2, 1] = to_row(total)
        xs(k).start()

    def step(k, carry):
        send_core(k + 1)
        compute(k)

        @pl.when((k >= 1) & (k < 3))
        def _():
            route_y(k - 1)

        @pl.when(k >= 3)
        def _():
            route_x(k - 1)

        return carry

    send_core(1)
    cr().wait_recv()
    compute(0)
    lax.fori_loop(1, 7, step, 0)

    parts = [half_parts(y_out[y], y_ost[y])]
    for d in (1, 2, 3):
        ys(d).wait_recv()
        parts.append(half_parts(y_in[d - 1], y_ist[d - 1]))
    rows, top, total = merge(parts)
    v_out[...] = rows.astype(jnp.bfloat16)
    v_ost[...] = to_row(top) + to_row(total, 64)
    vs().start()

    compute(7)

    def own_pair(k, j):
        parts = [core_merged(k)]
        for side in range(2):
            xr(side, j).wait_recv()
            rows = x_in[side, j].astype(jnp.float32)
            parts.append((rows, to_column(x_ist[side, j, 0], 128), to_column(x_ist[side, j, 1], 128)))
        return merge(parts)

    merged = own_pair(6, 1 - my_j)
    for t in range(QTOK):
        w_out[t], w_ost[t] = half_rows(merged, t)
        ws(t).start()

    def owner_rows(column, rows, top, total):
        rows = rows.reshape(8, 8, 512)
        z_out[column] = jnp.concatenate([rows[:, :, :256], rows[:, :, 256:]], axis=1).astype(jnp.bfloat16)
        lane, row = lanes((64, 128)), iota((64, 128), 0) % 8
        stats = jnp.where(lane == row, top, jnp.where(lane == row + 8, total, 0.0))
        z_ost[column] = jnp.sum(stats.reshape(8, 8, 128), axis=1, keepdims=True)

    merged = own_pair(7, my_j)
    even = y % 2 == 0
    tokens = [[token(a, t) for a in merged] for t in range(QTOK)]
    owner_rows(1, *[jnp.where(even, b, a) for a, b in zip(*tokens)])
    for d in (4, 3, 5, 2, 6, 1, 7, 0):
        zs(1, d).start()
    parts = [tuple(jnp.where(even, a, b) for a, b in zip(*tokens))]
    vs().wait_recv()
    parts.append(half_parts(v_in[...], v_ist[...]))
    for s in range(2):
        wr(s).wait_recv()
        parts.append(half_parts(w_in[s], w_ist[s]))
    owner_rows(0, *merge(parts))
    for d in z_order:
        zs(0, d).start()
    z_in[0, z] = z_out[0, z]
    z_ist[0, z] = z_ost[0, z]

    for d in range(1, NZ):
        rz(d).wait_send()
    for d in (1, 2, 3):
        rx(d).wait_send()
        ys(d).wait_send()
    cr().wait_send()
    vs().wait_send()
    for t in range(QTOK):
        ws(t).wait_send()

    def drain(p, carry):
        for j in range(2):
            for d in range(1, NZ):
                zq(p, j, d).wait_send()
            for d in (1, 2, 3):
                pq(p, j, d).wait_send()
            cq(p, j).wait_send()
            ce(p * 2 + j).wait_send()
        xs(p + 2).wait_send()
        return carry

    lax.fori_loop(0, 4, drain, 0)

    for d in range(1, NZ):
        zr(0, d).wait_recv()
    for d in range(NZ):
        zr(1, d).wait_recv()

    got = z_in[...].reshape(16, 16, 256).astype(jnp.float32)
    stats = jnp.broadcast_to(z_ist[...].reshape(16, 1, 128), (16, 8, 128))
    lane, row = lanes((16, 8, 128)), iota((16, 8, 128), 1)
    tops = jnp.sum(jnp.where(lane == row, stats, 0.0), axis=2, keepdims=True)
    totals = jnp.sum(jnp.where(lane == row + 8, stats, 0.0), axis=2, keepdims=True)
    factor = jnp.exp2(tops - jnp.max(tops, axis=0, keepdims=True))
    total = jnp.sum(totals * factor, axis=0)
    left = jnp.sum(got[:, :8] * factor, axis=0)
    right = jnp.sum(got[:, 8:] * factor, axis=0)
    out[...] = (jnp.concatenate([left, right], axis=1) / total).astype(jnp.bfloat16)

    for d in range(1, NZ):
        zs(0, d).wait_send()
    for d in range(NZ):
        zs(1, d).wait_send()


def body(latent_cache, rope_cache, q_latent, q_rope, lengths):
    _, positions, width = latent_cache.shape
    q_pairs = q_latent.reshape(4, 2, *q_latent.shape[1:])
    anywhere = pl.BlockSpec(memory_space=pl.ANY)
    dma = pltpu.SemaphoreType.DMA
    vmem, bf16, f32 = pltpu.VMEM, jnp.bfloat16, jnp.float32
    return pl.pallas_call(
        kernel,
        out_shape=jax.ShapeDtypeStruct((8, width), jnp.bfloat16),
        in_specs=[anywhere] * 4 + [pl.BlockSpec(memory_space=pltpu.SMEM)],
        out_specs=pl.BlockSpec(memory_space=pltpu.VMEM),
        scratch_shapes=[
            vmem((8, positions, width), bf16),
            vmem((8, 128, positions), bf16),
            vmem((4, 2, NZ, QTOK, 16, width), bf16),
            vmem((QTOK, 1024), bf16),
            vmem((2, 4, NZ, 16, 128), bf16),
            vmem((8, 2, 128, 640), f32),
            vmem((8, 128, 640), f32),
            vmem((4, 128, width), bf16), vmem((4, 2, 1, 128), f32),
            vmem((2, 2, 128, width), bf16), vmem((2, 2, 2, 1, 128), f32),
            vmem((4, 64, width), bf16), vmem((4, 1, 128), f32),
            vmem((3, 64, width), bf16), vmem((3, 1, 128), f32),
            vmem((64, width), bf16), vmem((1, 128), f32),
            vmem((64, width), bf16), vmem((1, 128), f32),
            vmem((2, 64, width), bf16), vmem((2, 1, 128), f32),
            vmem((2, 64, width), bf16), vmem((2, 1, 128), f32),
            vmem((2, 8, 16, 256), bf16), vmem((2, 8, 1, 128), f32),
            vmem((2, 8, 16, 256), bf16), vmem((2, 8, 1, 128), f32),
            dma((8, 3)), dma((3,)),
            dma((4, 2, 7)), dma((4, 2, 7)), dma((7,)), dma((7,)),
            dma((4, 2, 3)), dma((4, 2, 3)), dma((3,)), dma((3,)),
            dma((4, 2)), dma((4, 2)), dma, dma,
            dma((8,)), dma((8,)),
            dma((2, 4)), dma((2, 2, 2)), dma((2, 3)), dma((2, 3)), dma((2,)), dma((2,)),
            dma((2, 2)), dma((2, 2)), dma((2, 2, 8)), dma((2, 2, 8)),
        ],
        compiler_params=pltpu.CompilerParams(
            collective_id=0, has_side_effects=True, vmem_limit_bytes=56 * 2**20
        ),
        cost_estimate=pl.CostEstimate(flops=5 * 10**9, bytes_accessed=10 * 10**6, transcendentals=2 * 10**6),
    )(latent_cache, rope_cache, q_pairs, q_rope, lengths)


def solution(mesh):
    in_specs = (
        P(None, ("ctx", "sub"), None),
        P(None, None, ("ctx", "sub")),
        P(None, None, "sub", None),
        P(None, None, "sub"),
        P(),
    )
    out_specs = P(("ctx", "sub"), None)
    return jax.shard_map(body, mesh=mesh, in_specs=in_specs, out_specs=out_specs, check_vma=False)
```

time: 60 us -> 50.1 us (0.84)
  the two profiles are of different devices: /device:TPU:24 before, /device:TPU:1 now
where the time goes in v2:
time: 50.1 us; the launch traced here: 49.9 us
  Pallas kernels  48.6 us (97%)
  local copies, waits for them, and re-layouts  1.3 us (3%)
    pallas_call x1, Pallas kernels, body(): pl.pallas_call(kernel, out_shape=jax.ShapeDtypeStruct((8, width), jnp.bfl...  48.6 us
    unnamed x1, local copies, waits for them, and re-layouts  1.3 us

profile of v2, /device:TPU:1, one launch (start us, length us, event | category | flops | bytes accessed | tf_op | source)
XLA Modules:
  0.0 49.9 jit_solution(18343358168183745039)
XLA Ops:
  0.0 48.6 %shard_map.55 = bf16[8,512]{1,0:T(8,128)(2,1)} custom-call(bf16[8,1024,512]{2,1,0:T(8,128)(2,1)} %lat_hbm.1, bf16[8,64,1024]{2,1,0:T(8,128)(2,1)} %rope_hbm.1, bf16[4,2,2,16,512]{4,3,2,1,0:T(8,128)(2,1)} %bitcast.1, bf16[8,2,1024]{2,1,0:T(2,128)(2,1)} %qr_hbm.1, s32[8]{0:T(128)} %lengths.1), custom_call_target="tpu_custom_call" | custom-call | flops 5000000000 | bytes 10000000 | tf_op jit(solution)/shard_map/pallas_call | solution.py:486
  48.6 1.3 %copy.7 = bf16[8,512]{1,0:T(8,128)(2,1)} copy(bf16[8,512]{1,0:T(8,128)(2,1)} %shard_map.55) | data formatting | bytes 16384

commit v3 on v2

--- a/solution.py
+++ b/solution.py
@@ -269,7 +269,7 @@
             zq(p, j, d).wait_recv()
 
     send_z(wrap_x(2), 0)
-    for dx in pair_order:
+    for dx in (1, 3, 0, 2):
         send_z(wrap_x(dx), 1)
     for dx in pair_order[1:]:
         send_z(wrap_x(dx), 0)
@@ -283,11 +283,15 @@
     wait_z(wrap_x(2), 0)
     for d in (2, 1, 3):
         pq(wrap_x(2), 0, d).start()
-    for dx in pair_order:
+    for dx, ready in (
+        (1, ((1, 3),)),
+        (3, ((3, 1),)),
+        (0, ((0, 2), (0, 3), (3, 2))),
+        (2, ((2, 1), (1, 2), (0, 1), (2, 3), (1, 1), (3, 3), (2, 2))),
+    ):
         wait_z(wrap_x(dx), 1)
-    for dx in pair_order:
-        for d in (2, 1, 3):
-            pq(wrap_x(d + dx), 1, d).start()
+        for pair, d in ready:
+            pq(wrap_x(pair), 1, d).start()
     for dx in pair_order[1:]:
         wait_z(wrap_x(dx), 0)
         for d in (2, 1, 3):

time: 50.1 us -> 49.5 us (0.988)
  Pallas kernels: 48.6 us -> 48 us
    pallas_call x1, Pallas kernels: 48.6 us -> 48 us  [body(): pl.pallas_call(kernel, out_shape=jax.ShapeDtypeStruct((8, width), jnp.bfl...]
where the time goes in v3:
time: 49.5 us; the launch traced here: 49.3 us
  Pallas kernels  48 us (97%)
  local copies, waits for them, and re-layouts  1.3 us (3%)
    pallas_call x1, Pallas kernels, body(): pl.pallas_call(kernel, out_shape=jax.ShapeDtypeStruct((8, width), jnp.bfl...  48 us
    unnamed x1, local copies, waits for them, and re-layouts  1.3 us

profile of v3, /device:TPU:1, one launch (start us, length us, event | category | flops | bytes accessed | tf_op | source)
XLA Modules:
  0.0 49.3 jit_solution(18315269122252183320)
XLA Ops:
  0.0 48.0 %shard_map.55 = bf16[8,512]{1,0:T(8,128)(2,1)} custom-call(bf16[8,1024,512]{2,1,0:T(8,128)(2,1)} %lat_hbm.1, bf16[8,64,1024]{2,1,0:T(8,128)(2,1)} %rope_hbm.1, bf16[4,2,2,16,512]{4,3,2,1,0:T(8,128)(2,1)} %bitcast.1, bf16[8,2,1024]{2,1,0:T(2,128)(2,1)} %qr_hbm.1, s32[8]{0:T(128)} %lengths.1), custom_call_target="tpu_custom_call" | custom-call | flops 5000000000 | bytes 10000000 | tf_op jit(solution)/shard_map/pallas_call | solution.py:490
  48.0 1.3 %copy.7 = bf16[8,512]{1,0:T(8,128)(2,1)} copy(bf16[8,512]{1,0:T(8,128)(2,1)} %shard_map.55) | data formatting | bytes 16384

commit v4 on v3

--- a/solution.py
+++ b/solution.py
@@ -387,6 +387,28 @@
     compute(0)
     lax.fori_loop(1, 7, step, 0)
 
+    compute(7)
+
+    def own_pair(k, j):
+        parts = [core_merged(k)]
+        for side in range(2):
+            xr(side, j).wait_recv()
+            rows = x_in[side, j].astype(jnp.float32)
+            parts.append((rows, to_column(x_ist[side, j, 0], 128), to_column(x_ist[side, j, 1], 128)))
+        return merge(parts)
+
+    merged = own_pair(6, 1 - my_j)
+    for t in range(QTOK):
+        w_out[t], w_ost[t] = half_rows(merged, t)
+        ws(t).start()
+
+    def owner_rows(column, rows, top, total):
+        rows = rows.reshape(8, 8, 512)
+        z_out[column] = jnp.concatenate([rows[:, :, :256], rows[:, :, 256:]], axis=1).astype(jnp.bfloat16)
+        lane, row = lanes((64, 128)), iota((64, 128), 0) % 8
+        stats = jnp.where(lane == row, top, jnp.where(lane == row + 8, total, 0.0))
+        z_ost[column] = jnp.sum(stats.reshape(8, 8, 128), axis=1, keepdims=True)
+
     parts = [half_parts(y_out[y], y_ost[y])]
     for d in (1, 2, 3):
         ys(d).wait_recv()
@@ -395,28 +417,6 @@
     v_out[...] = rows.astype(jnp.bfloat16)
     v_ost[...] = to_row(top) + to_row(total, 64)
     vs().start()
-
-    compute(7)
-
-    def own_pair(k, j):
-        parts = [core_merged(k)]
-        for side in range(2):
-            xr(side, j).wait_recv()
-            rows = x_in[side, j].astype(jnp.float32)
-            parts.append((rows, to_column(x_ist[side, j, 0], 128), to_column(x_ist[side, j, 1], 128)))
-        return merge(parts)
-
-    merged = own_pair(6, 1 - my_j)
-    for t in range(QTOK):
-        w_out[t], w_ost[t] = half_rows(merged, t)
-        ws(t).start()
-
-    def owner_rows(column, rows, top, total):
-        rows = rows.reshape(8, 8, 512)
-        z_out[column] = jnp.concatenate([rows[:, :, :256], rows[:, :, 256:]], axis=1).astype(jnp.bfloat16)
-        lane, row = lanes((64, 128)), iota((64, 128), 0) % 8
-        stats = jnp.where(lane == row, top, jnp.where(lane == row + 8, total, 0.0))
-        z_ost[column] = jnp.sum(stats.reshape(8, 8, 128), axis=1, keepdims=True)
 
     merged = own_pair(7, my_j)
     even = y % 2 == 0

time: 49.5 us -> 48.9 us (0.988)
  Pallas kernels: 48 us -> 47.4 us
    pallas_call x1, Pallas kernels: 48 us -> 47.4 us  [body(): pl.pallas_call(kernel, out_shape=jax.ShapeDtypeStruct((8, width), jnp.bfl...]
where the time goes in v4:
time: 48.9 us; the launch traced here: 48.7 us
  Pallas kernels  47.4 us (97%)
  local copies, waits for them, and re-layouts  1.3 us (3%)
    pallas_call x1, Pallas kernels, body(): pl.pallas_call(kernel, out_shape=jax.ShapeDtypeStruct((8, width), jnp.bfl...  47.4 us
    unnamed x1, local copies, waits for them, and re-layouts  1.3 us

profile of v4, /device:TPU:1, one launch (start us, length us, event | category | flops | bytes accessed | tf_op | source)
XLA Modules:
  0.0 48.7 jit_solution(8395473858935725771)
XLA Ops:
  0.0 47.4 %shard_map.55 = bf16[8,512]{1,0:T(8,128)(2,1)} custom-call(bf16[8,1024,512]{2,1,0:T(8,128)(2,1)} %lat_hbm.1, bf16[8,64,1024]{2,1,0:T(8,128)(2,1)} %rope_hbm.1, bf16[4,2,2,16,512]{4,3,2,1,0:T(8,128)(2,1)} %bitcast.1, bf16[8,2,1024]{2,1,0:T(2,128)(2,1)} %qr_hbm.1, s32[8]{0:T(128)} %lengths.1), custom_call_target="tpu_custom_call" | custom-call | flops 5000000000 | bytes 10000000 | tf_op jit(solution)/shard_map/pallas_call | solution.py:490
  47.4 1.3 %copy.7 = bf16[8,512]{1,0:T(8,128)(2,1)} copy(bf16[8,512]{1,0:T(8,128)(2,1)} %shard_map.55) | data formatting | bytes 16384

commit v5 on v4

--- a/solution.py
+++ b/solution.py
@@ -257,9 +257,6 @@
 
     z_order = (4, 3, 5, 2, 6, 1, 7)
     pair_order = (2, 1, 3, 0)
-    for d in z_order:
-        rz(d).start()
-
     def send_z(p, j):
         for d in z_order:
             zq(p, j, d).start()
@@ -269,6 +266,8 @@
             zq(p, j, d).wait_recv()
 
     send_z(wrap_x(2), 0)
+    for d in z_order:
+        rz(d).start()
     for dx in (1, 3, 0, 2):
         send_z(wrap_x(dx), 1)
     for dx in pair_order[1:]:
@@ -276,13 +275,13 @@
     for copy in own_q:
         copy.wait()
 
+    wait_z(wrap_x(2), 0)
+    for d in (2, 1, 3):
+        pq(wrap_x(2), 0, d).start()
     for d in z_order:
         rz(d).wait_recv()
     for d in (2, 1, 3):
         rx(d).start()
-    wait_z(wrap_x(2), 0)
-    for d in (2, 1, 3):
-        pq(wrap_x(2), 0, d).start()
     for dx, ready in (
         (1, ((1, 3),)),
         (3, ((3, 1),)),

time: 48.9 us -> 49.2 us (level)
  no operation moved by 1% of the time
where the time goes in v5:
time: 49.2 us; the launch traced here: 49 us
  Pallas kernels  47.7 us (97%)
  local copies, waits for them, and re-layouts  1.3 us (3%)
    pallas_call x1, Pallas kernels, body(): pl.pallas_call(kernel, out_shape=jax.ShapeDtypeStruct((8, width), jnp.bfl...  47.7 us
    unnamed x1, local copies, waits for them, and re-layouts  1.3 us

profile of v5, /device:TPU:1, one launch (start us, length us, event | category | flops | bytes accessed | tf_op | source)
XLA Modules:
  0.0 49.0 jit_solution(4009912068893594838)
XLA Ops:
  0.0 47.7 %shard_map.55 = bf16[8,512]{1,0:T(8,128)(2,1)} custom-call(bf16[8,1024,512]{2,1,0:T(8,128)(2,1)} %lat_hbm.1, bf16[8,64,1024]{2,1,0:T(8,128)(2,1)} %rope_hbm.1, bf16[4,2,2,16,512]{4,3,2,1,0:T(8,128)(2,1)} %bitcast.1, bf16[8,2,1024]{2,1,0:T(2,128)(2,1)} %qr_hbm.1, s32[8]{0:T(128)} %lengths.1), custom_call_target="tpu_custom_call" | custom-call | flops 5000000000 | bytes 10000000 | tf_op jit(solution)/shard_map/pallas_call | solution.py:489
  47.7 1.3 %copy.7 = bf16[8,512]{1,0:T(8,128)(2,1)} copy(bf16[8,512]{1,0:T(8,128)(2,1)} %shard_map.55) | data formatting | bytes 16384
